TPU v7x, 256 devices: a whole 4x4x8 slice. The times are simulated.
256 devices in a mesh: mass: 8 (over x, core), seq: 32 (over y, z).
Axes of the slice: x: 4, y: 4, z: 8, core: 2. Of those that a mesh axis runs over, the one named last changes fastest.
Arguments:
- peptide_tokens: int32 [16384, 32], P(('mass', 'seq')), may hold values from 0 to 31
- peptide_lengths: int32 [16384], P(('mass', 'seq')), may hold values from 7 to 32
- target_owner: int32 [16384, 1], P(('mass', 'seq')), may hold values from 0 to 7; in each aligned block of 64 rows (0 to 63, 64 to 127, ...) at most 16 rows name the same one
- target_sub: int32 [16384], P(('mass', 'seq')), may hold values from 0 to 255
- decoy_owner: int32 [16384, 1], P(('mass', 'seq')), may hold values from 0 to 7; in each aligned block of 64 rows (0 to 63, 64 to 127, ...) at most 16 rows name the same one
- decoy_sub: int32 [16384], P(('mass', 'seq')), may hold values from 0 to 255
- embedding: bfloat16 [32, 256], replicated, may hold values from -6 to 6
- w_qkv: bfloat16 [2, 256, 768], replicated, may hold values from -2 to 2
- w_out: bfloat16 [2, 256, 256], replicated, may hold values from -0.375 to 0.375
- w_up: bfloat16 [2, 256, 1024], replicated, may hold values from -0.375 to 0.375
- w_down: bfloat16 [2, 1024, 256], replicated, may hold values from -0.1875 to 0.1875
- layer_gain: bfloat16 [2, 2, 256], replicated, may hold values from 0.5 to 1.5
- final_gain: bfloat16 [256], replicated, may hold values from 0.5 to 1.5
- w_head: bfloat16 [256, 32], replicated, may hold values from -0.375 to 0.375
- query_spectra: bfloat16 [8192, 1024], P(('mass', 'seq')), may hold values from -6 to 6
- query_bin: int32 [8192], P(('mass', 'seq')), may hold values from 0 to 2047, as said below
Outputs:
- target_best: float32 [8192], P(('mass', 'seq'))
- decoy_best: float32 [8192], P(('mass', 'seq'))
Inputs may be any that keep to these rules, and one draw needn't show every extreme that they name: `target_owner`: among the rows of one device at most 16 name the same owner. `decoy_owner`: among the rows of one device at most 16 name the same owner. `query_bin`: queries d * 32 to (d + 1) * 32 - 1 hold the bins d * 8 to (d + 1) * 8 - 1, each exactly 4 times.
All inputs are finite; a program needn't handle non-finite values.
Results may differ from a plain program's by a relative error of at most 0.0055.
Values may be sent and summed in bfloat16 or wider, within the bound.
No kernel may reach another device: no remote copies, remote signals or barrier semaphores. Data moves between devices by JAX's collectives and lax.ppermute only.
A program may use at most 128 MiB of HBM per device.

v0:
```python
import math

import jax
import jax.numpy as jnp
from jax import lax
from jax.sharding import PartitionSpec as P

HEADS = 8
L = 32
ION = 32
NL = 2
QPB = 4


EPS = 1e-06


def sinusoid(length, width):
    place = jnp.arange(length, dtype=jnp.float32)[:, None]
    index = jnp.arange(width // 2, dtype=jnp.float32)[None, :]
    angle = place * jnp.exp(-math.log(10000.0) * 2.0 * index / width)
    return jnp.concatenate([jnp.sin(angle), jnp.cos(angle)], axis=1)


def norm_rows(values, gain):
    return (
        values
        * lax.rsqrt(jnp.mean(values * values, axis=-1, keepdims=True) + EPS)
        * gain.astype(jnp.float32)
    )


def standardize(spectra):
    centred = spectra - jnp.mean(spectra, axis=-1, keepdims=True)
    return (centred * lax.rsqrt(jnp.mean(centred * centred, axis=-1, keepdims=True) + EPS)).astype(
        jnp.bfloat16
    )


def predict_block(
    tokens, lengths, embedding, w_qkv, w_out, w_up, w_down, layer_gain, final_gain, w_head
):
    count, length = tokens.shape
    vocab, width = embedding.shape
    size = width // HEADS
    onehot = (tokens.reshape(-1)[:, None] == jnp.arange(vocab, dtype=jnp.int32)[None, :]).astype(
        jnp.bfloat16
    )
    state = jnp.dot(onehot, embedding, preferred_element_type=jnp.float32).reshape(
        count, length, width
    )
    state = (state + sinusoid(length, width)[None]).reshape(count * length, width)
    valid = jnp.arange(length, dtype=jnp.int32)[None, :] < lengths[:, None]
    for layer in range(NL):
        normed = norm_rows(state, layer_gain[layer, 0]).astype(jnp.bfloat16)
        mixed = jnp.dot(normed, w_qkv[layer], preferred_element_type=jnp.float32).astype(
            jnp.bfloat16
        )
        mixed = mixed.reshape(count, length, 3, HEADS, size)
        scores = jnp.einsum(
            "pqhe,pkhe->phqk", mixed[:, :, 0], mixed[:, :, 1], preferred_element_type=jnp.float32
        ) / math.sqrt(size)
        scores = jnp.where(valid[:, None, None, :], scores, jnp.float32(-1e30))
        top = jnp.max(scores, axis=-1, keepdims=True)
        weights = jnp.exp(scores - top)
        probs = (weights / jnp.sum(weights, axis=-1, keepdims=True)).astype(jnp.bfloat16)
        attended = jnp.einsum(
            "phqk,pkhe->pqhe", probs, mixed[:, :, 2], preferred_element_type=jnp.float32
        ).astype(jnp.bfloat16)
        attended = attended.reshape(count * length, width)
        state = state + jnp.dot(attended, w_out[layer], preferred_element_type=jnp.float32)
        normed = norm_rows(state, layer_gain[layer, 1]).astype(jnp.bfloat16)
        hidden = jax.nn.gelu(
            jnp.dot(normed, w_up[layer], preferred_element_type=jnp.float32), approximate=True
        ).astype(jnp.bfloat16)
        state = state + jnp.dot(hidden, w_down[layer], preferred_element_type=jnp.float32)
    normed = norm_rows(state, final_gain).astype(jnp.bfloat16)
    intensity = jax.nn.sigmoid(jnp.dot(normed, w_head, preferred_element_type=jnp.float32)).reshape(
        count, length, -1
    )
    fragment = jnp.arange(length, dtype=jnp.int32)[None, :] < lengths[:, None] - 1
    intensity = jnp.where(fragment[:, :, None], intensity, jnp.float32(0.0))
    return standardize(intensity.reshape(count, -1))


def pack_rows(rows, owner, global_bins, capacity, masses):
    member = (owner[:, None] == jnp.arange(masses, dtype=jnp.int32)[None, :]).astype(jnp.int32)
    rank = jnp.sum((jnp.cumsum(member, axis=0) - member) * member, axis=1)
    slot = owner * capacity + rank
    place = slot[None, :] == jnp.arange(masses * capacity, dtype=jnp.int32)[:, None]
    packed = jnp.dot(place.astype(jnp.bfloat16), rows, preferred_element_type=jnp.float32).astype(
        jnp.bfloat16
    )
    packed_bins = jnp.sum(jnp.where(place, global_bins[None, :] + 1, 0), axis=1) - 1
    return (packed.reshape(masses, capacity, rows.shape[1]), packed_bins.reshape(masses, capacity))


def best_match(queries, query_bins, rows, row_bins):
    scores = lax.dot_general(
        queries, rows, (((1,), (1,)), ((), ())), preferred_element_type=jnp.float32
    )
    scores = scores / math.sqrt(queries.shape[1])
    matched = query_bins[:, None] == row_bins[None, :]
    return jnp.max(jnp.where(matched, scores, jnp.float32(0.0)), axis=1)


def local(
    peptide_tokens,
    peptide_lengths,
    target_owner,
    target_sub,
    decoy_owner,
    decoy_sub,
    embedding,
    w_qkv,
    w_out,
    w_up,
    w_down,
    layer_gain,
    final_gain,
    w_head,
    query_spectra,
    query_bin,
):
    masses = lax.axis_size("mass")
    seqs = lax.axis_size("seq")
    count = peptide_tokens.shape[0]
    queries_dev = query_spectra.shape[0]
    spec_bins = query_spectra.shape[1]
    bin_dev = queries_dev * seqs // QPB
    capacity = max(2, 2 * count // masses)
    rows = predict_block(
        peptide_tokens,
        peptide_lengths,
        embedding,
        w_qkv,
        w_out,
        w_up,
        w_down,
        layer_gain,
        final_gain,
        w_head,
    )
    decoys = rows.reshape(count, L, ION)[:, ::-1, :].reshape(count, spec_bins)
    target_global = target_owner[:, 0] * bin_dev + target_sub
    decoy_global = decoy_owner[:, 0] * bin_dev + decoy_sub
    target_packed, target_packed_bins = pack_rows(
        rows, target_owner[:, 0], target_global, capacity, masses
    )
    decoy_packed, decoy_packed_bins = pack_rows(
        decoys, decoy_owner[:, 0], decoy_global, capacity, masses
    )
    target_rows, target_bins, decoy_rows, decoy_bins = (
        lax.all_to_all(target_packed, "mass", split_axis=0, concat_axis=0, tiled=True),
        lax.all_to_all(target_packed_bins, "mass", split_axis=0, concat_axis=0, tiled=True),
        lax.all_to_all(decoy_packed, "mass", split_axis=0, concat_axis=0, tiled=True),
        lax.all_to_all(decoy_packed_bins, "mass", split_axis=0, concat_axis=0, tiled=True),
    )
    target_rows = target_rows.reshape(masses * capacity, spec_bins)
    decoy_rows = decoy_rows.reshape(masses * capacity, spec_bins)
    target_bins = target_bins.reshape(masses * capacity)
    decoy_bins = decoy_bins.reshape(masses * capacity)
    queries = standardize(query_spectra.astype(jnp.float32))
    zeros = jnp.zeros((queries_dev,), jnp.float32)
    target_piece = best_match(
        queries,
        query_bin,
        lax.all_gather(target_rows, "seq", axis=0, tiled=True),
        lax.all_gather(target_bins, "seq", axis=0, tiled=True),
    )
    decoy_piece = best_match(
        queries,
        query_bin,
        lax.all_gather(decoy_rows, "seq", axis=0, tiled=True),
        lax.all_gather(decoy_bins, "seq", axis=0, tiled=True),
    )
    target_best = jnp.maximum(zeros, target_piece)
    decoy_best = jnp.maximum(zeros, decoy_piece)
    return (target_best, decoy_best)


def solution(mesh):
    in_specs = (
        P(("mass", "seq"), None),
        P(("mass", "seq")),
        P(("mass", "seq"), None),
        P(("mass", "seq")),
        P(("mass", "seq"), None),
        P(("mass", "seq")),
        P(),
        P(),
        P(),
        P(),
        P(),
        P(),
        P(),
        P(),
        P(("mass", "seq"), None),
        P(("mass", "seq")),
    )
    out_specs = (P(("mass", "seq")), P(("mass", "seq")))
    return jax.shard_map(local, mesh=mesh, in_specs=in_specs, out_specs=out_specs, check_vma=False)
```

profile of v0, /device:TPU:1, one launch (start us, length us, event | category | flops | bytes accessed | tf_op | source)
XLA Modules:
  0.0 376.4 jit_solution(8750267194502979055)
XLA Ops:
  7.2 0.7 iota_compare_fusion.4
  8.0 0.7 broadcast_add_fusion
  8.7 0.2 add.155
  9.0 1.9 copy.63
  11.1 2.2 multiply_reduce_fusion.4
  13.3 2.8 convolution_convert_fusion.1
  16.1 14.9 %reshape.279 = bf16[64,32,3,8,32]{4,3,2,1,0:T(8,128)(2,1)} reshape(bf16[2048,768]{1,0:T(8,128)(2,1)} %convolution_convert_fusion.1) | data formatting | bytes 6291456 | tf_op jit(solution)/shard_map/reshape | solution.py:59
  31.0 8.9 %fusion.123 = (bf16[64,32,1,8,32]{4,3,2,1,0:T(8,128)(2,1)}, bf16[64,32,1,8,32]{4,3,2,1,0:T(8,128)(2,1)}, bf16[64,32,1,8,32]{4,3,2,1,0:T(8,128)(2,1)}) fusion(bf16[64,32,3,8,32]{4,3,2,1,0:T(8,128)(2,1)} %reshape.279), kind=kLoop, calls=%fused_computation.175 | loop fusion | bytes 6291456 | tf_op jit(solution)/shard_map/slice | solution.py:68
  39.9 6.6 %copy.80 = bf16[64,32,1,8,32]{1,4,3,0,2:T(8,128)(2,1)} copy(bf16[64,32,1,8,32]{4,3,2,1,0:T(8,128)(2,1)} %get-tuple-element.5) | data formatting | bytes 2097152
  46.5 5.8 %fusion.25 = f32[64,8,32,32]{2,3,1,0:T(8,128)S(1)} fusion(bf16[64,32,1,8,32]{4,3,2,1,0:T(8,128)(2,1)} %get-tuple-element.6, bf16[64,32,1,8,32]{4,3,2,1,0:T(8,128)(2,1)} %get-tuple-element.7), kind=kOutput, calls=%fused_computation.38 | convolution fusion | flops 33554432 | bytes 4194304 | tf_op jit(solution)/shard_map/pqhe,pkhe->phqk/dot_general | solution.py:60
  52.3 6.0 %fusion.124 = (f32[64,8,32]{2,1,0:T(8,128)S(1)}, f32[64,8,32,32]{2,3,1,0:T(8,128)}) fusion(f32[64,8,32,32]{2,3,1,0:T(8,128)S(1)} %fusion.25, pred[64,32]{1,0:T(8,128)(4,1)S(1)} %iota_compare_fusion.4), kind=kOutput, calls=%fused_computation.176 | output fusion | flops 3145759 | bytes 4261888 | tf_op jit(solution)/shard_map/sub | solution.py:65
  58.3 6.7 %convert_bitcast_fusion.1 = bf16[64,32,8,32]{1,3,2,0:T(8,128)(2,1)} fusion(f32[64,8,32,32]{2,3,1,0:T(8,128)} %get-tuple-element.21, f32[64,8,32]{2,1,0:T(8,128)S(1)} %get-tuple-element.20, bf16[64,32,1,8,32]{1,4,3,0,2:T(8,128)(2,1)S(1)} %copy-done.3), kind=kOutput, calls=%fused_computation.44 | convolution fusion | flops 35127296 | bytes 4259840 | tf_op jit(solution)/shard_map/phqk,pkhe->pqhe/dot_general | solution.py:67
  65.0 6.6 %copy.68 = bf16[64,32,8,32]{3,2,1,0:T(8,128)(2,1)} copy(bf16[64,32,8,32]{1,3,2,0:T(8,128)(2,1)} %convert_bitcast_fusion.1) | data formatting | bytes 2097152 | tf_op jit(solution)/shard_map/convert_element_type | solution.py:69
  71.6 5.6 %reshape.280 = bf16[2048,256]{1,0:T(8,128)(2,1)S(1)} reshape(bf16[64,32,8,32]{3,2,1,0:T(8,128)(2,1)} %copy.68) | data formatting | bytes 2097152 | tf_op jit(solution)/shard_map/reshape | solution.py:70
  77.1 1.8 multiply_reduce_fusion.3
  79.0 7.5 %multiply_reduce_fusion.2 = (f32[2048]{0:T(1024)S(1)}, f32[2048,256]{0,1:T(8,128)}) fusion(f32[2048,256]{0,1:T(8,128)} %get-tuple-element.23, bf16[2,1024,256]{2,1,0:T(8,128)(2,1)} %param.26, f32[256]{0:T(256)S(1)} %bitcast.115, f32[2048]{0:T(1024)S(1)} %add_rsqrt_fusion.3, bf16[2,256,1024]{2,1,0:T(8,128)(2,1)} %param.25), kind=kOutput, calls=%fused_computation.72 | convolution fusion | flops 2169501696 | bytes 7357440 | tf_op jit(solution)/shard_map/dot_general | solution.py:76
  86.5 2.7 convolution_convert_fusion
  89.3 10.0 %reshape.281 = bf16[64,32,3,8,32]{4,3,2,1,0:T(8,128)(2,1)} reshape(bf16[2048,768]{1,0:T(8,128)(2,1)S(1)} %convolution_convert_fusion) | data formatting | bytes 6291456 | tf_op jit(solution)/shard_map/reshape | solution.py:59
  99.2 7.1 %fusion.122 = (bf16[64,32,1,8,32]{4,3,2,1,0:T(8,128)(2,1)}, bf16[64,32,1,8,32]{4,3,2,1,0:T(8,128)(2,1)S(1)}, bf16[64,32,1,8,32]{4,3,2,1,0:T(8,128)(2,1)S(1)}) fusion(bf16[64,32,3,8,32]{4,3,2,1,0:T(8,128)(2,1)} %reshape.281), kind=kLoop, calls=%fused_computation.174 | loop fusion | bytes 6291456 | tf_op jit(solution)/shard_map/slice | solution.py:68
  106.4 2.3 fusion.24
  108.7 6.0 %fusion.127 = (f32[64,8,32]{2,1,0:T(8,128)S(1)}, f32[64,8,32,32]{2,3,1,0:T(8,128)}) fusion(f32[64,8,32,32]{2,3,1,0:T(8,128)S(1)} %fusion.24, pred[64,32]{1,0:T(8,128)(4,1)S(1)} %iota_compare_fusion.4), kind=kOutput, calls=%fused_computation.177 | output fusion | flops 3145759 | bytes 4261888 | tf_op jit(solution)/shard_map/sub | solution.py:65
  114.6 6.6 %copy.83 = bf16[64,32,1,8,32]{1,4,3,0,2:T(8,128)(2,1)} copy(bf16[64,32,1,8,32]{4,3,2,1,0:T(8,128)(2,1)} %get-tuple-element.2) | data formatting | bytes 2097152
  121.2 7.9 %convert_bitcast_fusion = bf16[64,32,8,32]{1,3,2,0:T(8,128)(2,1)} fusion(f32[64,8,32,32]{2,3,1,0:T(8,128)} %get-tuple-element.27, f32[64,8,32]{2,1,0:T(8,128)S(1)} %get-tuple-element.26, bf16[64,32,1,8,32]{1,4,3,0,2:T(8,128)(2,1)} %copy.83), kind=kOutput, calls=%fused_computation.42 | convolution fusion | flops 35127296 | bytes 4259840 | tf_op jit(solution)/shard_map/phqk,pkhe->pqhe/dot_general | solution.py:67
  129.1 6.6 %copy.73 = bf16[64,32,8,32]{3,2,1,0:T(8,128)(2,1)} copy(bf16[64,32,8,32]{1,3,2,0:T(8,128)(2,1)} %convert_bitcast_fusion) | data formatting | bytes 2097152 | tf_op jit(solution)/shard_map/convert_element_type | solution.py:69
  135.7 5.5 %reshape.282 = bf16[2048,256]{1,0:T(8,128)(2,1)S(1)} reshape(bf16[64,32,8,32]{3,2,1,0:T(8,128)(2,1)} %copy.73) | data formatting | bytes 2097152 | tf_op jit(solution)/shard_map/reshape | solution.py:70
  141.2 1.8 multiply_reduce_fusion.1
  143.1 6.2 %multiply_reduce_fusion = (f32[2048]{0:T(1024)S(1)}, f32[2048,256]{0,1:T(8,128)S(1)}) fusion(f32[2048,256]{0,1:T(8,128)} %get-tuple-element.29, bf16[2,1024,256]{2,1,0:T(8,128)(2,1)} %param.26, f32[256]{0:T(256)S(1)} %bitcast.114, f32[2048]{0:T(1024)S(1)} %add_rsqrt_fusion.1, bf16[2,256,1024]{2,1,0:T(8,128)(2,1)} %param.25), kind=kOutput, calls=%fused_computation.68 | convolution fusion | flops 2169501696 | bytes 7357440 | tf_op jit(solution)/shard_map/dot_general | solution.py:76
  149.5 0.4 select_reduce_fusion
  150.0 0.1 reduce_sum.162
  150.3 0.4 reshape.287
  150.8 0.1 reduce_sum.165
  150.9 0.3 multiply_convert_fusion.12
  151.2 0.4 rev.3
  151.6 0.4 copy.77
  152.2 0.1 reduce_window_sum.18
  152.3 0.2 select_reduce_fusion.2
  152.5 0.3 convolution_convert_fusion.2
  152.8 12.8 %all_to_all.22 = bf16[8,16,1024]{2,1,0:T(8,128)(2,1)} all-to-all(bf16[8,16,1024]{2,1,0:T(8,128)(2,1)S(1)} %bitcast.102), channel_id=1, replica_groups=mesh['mass'=8,'seq'=32] {'mass'}, dimensions={0} | all-to-all | bytes 524288 | tf_op jit(solution)/shard_map/all_to_all | solution.py:156
  165.7 0.3 copy.74
  166.1 0.5 reshape.283
  166.6 0.2 copy.75
  167.1 0.2 select_reduce_fusion.4
  167.3 0.3 convolution_convert_fusion.3
  167.6 10.6 %all_to_all.23 = bf16[8,16,1024]{2,1,0:T(8,128)(2,1)} all-to-all(bf16[8,16,1024]{2,1,0:T(8,128)(2,1)S(1)} %bitcast.103), channel_id=1, replica_groups=mesh['mass'=8,'seq'=32] {'mass'}, dimensions={0} | all-to-all | bytes 524288 | tf_op jit(solution)/shard_map/all_to_all | solution.py:154
  178.2 0.1 select_reduce_fusion.1
  178.3 0.7 sub.85
  179.0 4.3 %all-to-all-start.2 = ((s32[8,1,16]{2,1,0:T(1,128)}), s32[8,1,16]{2,1,0:T(1,128)S(1)}, u32[]{:S(2)}, u32[]{:S(2)}) async-start(s32[8,1,16]{2,1,0:T(1,128)} %bitcast.28), calls=%async_computation.2 | async-start | bytes 8192 | tf_op jit(solution)/shard_map/all_to_all | solution.py:157
  183.3 0.1 select_reduce_fusion.3
  183.4 0.1 convert_reduce_fusion
  183.5 0.2 fusion.92
  183.7 0.7 sub.69
  184.4 3.5 all-to-all-done.2
  187.9 3.8 %all-to-all-start = ((s32[8,1,16]{2,1,0:T(1,128)}), s32[8,1,16]{2,1,0:T(1,128)S(1)}, u32[]{:S(2)}, u32[]{:S(2)}) async-start(s32[8,1,16]{2,1,0:T(1,128)} %bitcast.1), calls=%async_computation | async-start | bytes 8192 | tf_op jit(solution)/shard_map/all_to_all | solution.py:155
  191.7 0.5 broadcast.340
  192.2 0.7 reduce.13
  193.0 3.4 all-to-all-done
  196.4 0.7 reduce.12
  197.1 35.6 %all-gather.1 = s32[32,1,128]{2,1,0:T(1,128)S(1)} all-gather(s32[1,1,128]{2,1,0:T(1,128)S(1)} %reshape.297), channel_id=1, replica_groups=mesh['mass'=8,'seq'=32] {'seq'}, dimensions={0}, use_global_device_ids=true | all-gather | bytes 16896 | tf_op jit(solution)/shard_map/all_gather | solution.py:175
  232.7 32.1 %all-gather = s32[32,1,128]{2,1,0:T(1,128)S(1)} all-gather(s32[1,1,128]{2,1,0:T(1,128)S(1)} %reshape.295), channel_id=1, replica_groups=mesh['mass'=8,'seq'=32] {'seq'}, dimensions={0}, use_global_device_ids=true | all-gather | bytes 16896 | tf_op jit(solution)/shard_map/all_gather | solution.py:169
  264.9 6.1 %fusion.58 = f32[32]{0:T(128)S(1)} fusion(bf16[4096,1024]{1,0:T(8,128)(2,1)} %all-gather.7.cloned.1.call-done, s32[4096]{0:T(1024)S(1)} %bitcast.107, s32[32]{0:T(128)S(1)} %copy-done.12, bf16[32,1024]{1,0:T(8,128)(2,1)S(1)} %copy-done.4, f32[32]{0:T(128)S(1)} %add_rsqrt_fusion.6, f32[32]{0:T(128)S(1)} %broadcast_multiply_fusion.1), kind=kOutput, calls=%fused_computation.80 | convolution fusion | flops 269090784 | bytes 8471040 | tf_op jit(solution)/shard_map/dot_general | solution.py:99
  271.0 0.5 broadcast_maximum_fusion
  271.5 91.4 %all-gather.5.cloned.1.call-done = bf16[4096,1024]{1,0:T(8,128)(2,1)} async-done(((bf16[128,1024]{1,0:T(8,128)(2,1)}), bf16[4096,1024]{1,0:T(8,128)(2,1)}) %all-gather.5.cloned.1.call-update) | async-done | bytes 8388624 | tf_op jit(solution)/shard_map/all_gather | solution.py:168
  362.9 6.1 %fusion.57 = f32[32]{0:T(128)S(1)} fusion(bf16[4096,1024]{1,0:T(8,128)(2,1)} %all-gather.5.cloned.1.call-done, s32[4096]{0:T(1024)S(1)} %bitcast.106, s32[32]{0:T(128)S(1)} %copy-done.12, bf16[32,1024]{1,0:T(8,128)(2,1)S(1)} %copy-done.4, f32[32]{0:T(128)S(1)} %add_rsqrt_fusion.6, f32[32]{0:T(128)S(1)} %broadcast_multiply_fusion.1), kind=kOutput, calls=%fused_computation.79 | convolution fusion | flops 269090784 | bytes 8471040 | tf_op jit(solution)/shard_map/dot_general | solution.py:99
  369.0 0.5 broadcast_maximum_fusion.1
  (71 shorter events, 1.6 us)
Async XLA Ops:
  7.2 3.9 %copy-start = (bf16[32,256]{1,0:T(8,128)(2,1)S(1)}, bf16[32,256]{1,0:T(8,128)(2,1)}, u32[]{:S(2)}) copy-start(bf16[32,256]{1,0:T(8,128)(2,1)} %param.22) | copy-start | bytes 49156
  7.2 3.7 copy-start.8
  7.2 257.7 %all-gather.7.cloned.1.call-start = ((), (), s32[]{:S(2)}) async-start(), calls=%async_computation.5 | async-start | bytes 8650752 | tf_op jit(solution)/shard_map/all_gather | solution.py:174
  9.0 4.3 %copy-start.9 = (bf16[2,2,256]{2,1,0:T(2,128)(2,1)S(1)}, bf16[2,2,256]{2,1,0:T(2,128)(2,1)}, u32[]{:S(2)}) copy-start(bf16[2,2,256]{2,1,0:T(2,128)(2,1)} %param.27) | copy-start | bytes 6148
  9.0 4.3 %copy-start.5 = (bf16[2,256,768]{2,1,0:T(8,128)(2,1)S(1)}, bf16[2,256,768]{2,1,0:T(8,128)(2,1)}, u32[]{:S(2)}) copy-start(bf16[2,256,768]{2,1,0:T(8,128)(2,1)} %param.23) | copy-start | bytes 2359300
  52.3 6.0 %copy-start.3 = (bf16[64,32,1,8,32]{1,4,3,0,2:T(8,128)(2,1)S(1)}, bf16[64,32,1,8,32]{1,4,3,0,2:T(8,128)(2,1)}, u32[]{:S(2)}) copy-start(bf16[64,32,1,8,32]{1,4,3,0,2:T(8,128)(2,1)} %copy.80) | copy-start | bytes 3145732
  71.6 5.6 %copy-start.6 = (bf16[2,256,256]{2,1,0:T(8,128)(2,1)S(1)}, bf16[2,256,256]{2,1,0:T(8,128)(2,1)}, u32[]{:S(2)}) copy-start(bf16[2,256,256]{2,1,0:T(8,128)(2,1)} %param.24) | copy-start | bytes 786436
  135.7 5.5 %copy-start.2 = (f32[2048,256]{0,1:T(8,128)S(1)}, f32[2048,256]{0,1:T(8,128)}, u32[]{:S(2)}) copy-start(f32[2048,256]{0,1:T(8,128)} %get-tuple-element.25) | copy-start | bytes 6291460
  143.1 6.4 %copy-start.15 = (bf16[256]{0:T(256)(128)(2,1)S(1)}, bf16[256]{0:T(256)(128)(2,1)}, u32[]{:S(2)}) copy-start(bf16[256]{0:T(256)(128)(2,1)} %param.28) | copy-start | bytes 1540
  143.1 6.4 %copy-start.7 = (bf16[256,32]{0,1:T(8,128)(2,1)S(1)}, bf16[256,32]{0,1:T(8,128)(2,1)}, u32[]{:S(2)}) copy-start(bf16[256,32]{0,1:T(8,128)(2,1)} %param.29) | copy-start | bytes 49156
  149.3 2.8 copy-start.10
  149.3 3.1 copy-start.13
  150.7 16.1 %copy-start.11 = (s32[64,1]{0,1:T(1,128)S(1)}, s32[64,1]{0,1:T(1,128)}, u32[]{:S(2)}) copy-start(s32[64,1]{0,1:T(1,128)} %param.18) | copy-start | bytes 772
  151.2 16.0 %copy-start.14 = (s32[64]{0:T(128)S(1)}, s32[64]{0:T(128)}, u32[]{:S(2)}) copy-start(s32[64]{0:T(128)} %param.19) | copy-start | bytes 772
  151.6 31.8 %copy-start.4 = (bf16[32,1024]{1,0:T(8,128)(2,1)S(1)}, bf16[32,1024]{1,0:T(8,128)(2,1)}, u32[]{:S(2)}) copy-start(bf16[32,1024]{1,0:T(8,128)(2,1)} %param.30) | copy-start | bytes 196612
  151.6 113.2 %copy-start.12 = (s32[32]{0:T(128)S(1)}, s32[32]{0:T(128)}, u32[]{:S(2)}) copy-start(s32[32]{0:T(128)} %param.31) | copy-start | bytes 388
  165.6 197.3 %all-gather.5.cloned.1.call-start = ((), (), s32[]{:S(2)}) async-start(), calls=%async_computation.4 | async-start | bytes 8650752 | tf_op jit(solution)/shard_map/all_gather | solution.py:168
  179.0 8.9 %all-to-all-start.2 = ((s32[8,1,16]{2,1,0:T(1,128)}), s32[8,1,16]{2,1,0:T(1,128)S(1)}, u32[]{:S(2)}, u32[]{:S(2)}) async-start(s32[8,1,16]{2,1,0:T(1,128)} %bitcast.28), calls=%async_computation.2 | async-start | bytes 8192 | tf_op jit(solution)/shard_map/all_to_all | solution.py:157
  187.9 8.5 %all-to-all-start = ((s32[8,1,16]{2,1,0:T(1,128)}), s32[8,1,16]{2,1,0:T(1,128)S(1)}, u32[]{:S(2)}, u32[]{:S(2)}) async-start(s32[8,1,16]{2,1,0:T(1,128)} %bitcast.1), calls=%async_computation | async-start | bytes 8192 | tf_op jit(solution)/shard_map/all_to_all | solution.py:155
  362.9 6.7 %copy-start.1 = (bf16[32,256]{1,0:T(8,128)(2,1)S(1)}, bf16[32,256]{1,0:T(8,128)(2,1)}, u32[]{:S(2)}) copy-start(bf16[32,256]{1,0:T(8,128)(2,1)} %param.22) | copy-start | bytes 49156
Sparse Core Ops, SparseCore 0:
  165.7 99.0 all-gather.6
  267.5 95.3 all-gather.4
where the time goes:
time: 378 us; the launch traced here: 376 us
  waiting for transfers between devices  98.3 us (26%)
  blocking collectives  91.1 us (24%)
  local copies, waits for them, and re-layouts  85.4 us (23%)
  matrix products  61.1 us (16%)
  other arithmetic  17.8 us (5%)
  between operations  14.5 us (4%)
  starting transfers between devices  8.2 us (2%)
    all_gather x1, waiting for transfers between devices, local(): lax.all_gather(target_rows, 'seq', axis=0, tiled=True)  91.4 us
    all_gather x1, blocking collectives, local(): lax.all_gather(decoy_bins, 'seq', axis=0, tiled=True)  35.6 us
    all_gather x1, blocking collectives, local(): lax.all_gather(target_bins, 'seq', axis=0, tiled=True)  32.1 us
    reshape x2, local copies, waits for them, and re-layouts, predict_block(): mixed = mixed.reshape(count, length, 3, HEADS, size)  24.9 us
    slice x2, local copies, waits for them, and re-layouts, predict_block(): mixed[:, :, 2]  16 us
    dot_general x2, matrix products, predict_block(): jnp.einsum('phqk,pkhe->pqhe', probs, mixed[:, :, 2], preferred_element_ty...  14.5 us
    dot_general x2, matrix products, predict_block(): jnp.dot(hidden, w_down[layer], preferred_element_type=jnp.float32)  13.7 us
    unnamed x38, local copies, waits for them, and re-layouts  13.6 us
  transfers between devices with their start and end apart: 4, of which 3 were waited for; matrix products, arithmetic and copies ran while one was open for 3% of the time, Pallas kernels for 0%

commit v1 on v0

v1 whole, which is shorter than its diff:
```python
import functools
import math

import jax
import jax.numpy as jnp
import numpy as np
from jax import lax
from jax.experimental import pallas as pl
from jax.experimental.pallas import tpu as pltpu
from jax.sharding import PartitionSpec as P

HEADS = 8
L = 32
ION = 32
NL = 2
QPB = 4
D = 256
FF = 1024
SPEC = L * ION
EPS = 1e-06
BF = jnp.bfloat16
F32 = jnp.float32

STEP = 256
TILE = 128
ROWW = SPEC + 128
NT = (((1,), (1,)), ((), ()))
TN = (((0,), (0,)), ((), ()))


def sinusoid():
    place = np.arange(L, dtype=np.float32)[:, None]
    index = np.arange(D // 2, dtype=np.float32)[None, :]
    angle = place * np.exp(-math.log(10000.0) * 2.0 * index / D).astype(np.float32)
    return np.concatenate([np.sin(angle), np.cos(angle)], axis=1).astype(np.float32)


def lane_iota(shape):
    return lax.broadcasted_iota(jnp.int32, shape, len(shape) - 1)


def row_iota(shape):
    return lax.broadcasted_iota(jnp.int32, shape, len(shape) - 2)


def norm_rows(values, gain):
    scale = lax.rsqrt(jnp.mean(values * values, axis=-1, keepdims=True) + EPS)
    return (values * scale * gain).astype(BF)


def standardize(spectra):
    centred = spectra - jnp.mean(spectra, axis=-1, keepdims=True)
    return (centred * lax.rsqrt(jnp.mean(centred * centred, axis=-1, keepdims=True) + EPS)).astype(BF)


def gelu(x):
    inner = x * (math.sqrt(2 / math.pi) + (math.sqrt(2 / math.pi) * 0.044715) * (x * x))
    half = 0.5 * x
    return half + half * jnp.tanh(inner)


def attend(q, k, v, length_lane):
    heads = TILE // L
    lane = lane_iota((TILE, TILE)) // L
    zero = jnp.zeros_like(q)
    spread = jnp.concatenate([jnp.where(lane == h, q, zero) for h in range(heads)], axis=0)
    scores = lax.dot_general(k, spread, NT, preferred_element_type=F32)
    lane4 = (lane_iota((L, heads * TILE)) % TILE) // L
    compact = scores[:L]
    for j in range(1, TILE // L):
        compact = jnp.where(lane4 == j, scores[j * L : (j + 1) * L], compact)
    compact = compact * (1.0 / math.sqrt(L))
    lengths = jnp.concatenate([length_lane] * heads, axis=1)
    compact = jnp.where(row_iota(compact.shape) < lengths, compact, F32(-1e30))
    weights = jnp.exp(compact - jnp.max(compact, axis=0, keepdims=True))
    probs = weights * (1.0 / jnp.sum(weights, axis=0, keepdims=True))
    probs = probs.astype(BF)
    wide = jnp.concatenate(
        [jnp.where(lane4 == j, probs, jnp.zeros_like(probs)) for j in range(TILE // L)], axis=0
    )
    turned = v.T
    out = jnp.concatenate(
        [
            jnp.dot(
                turned[h * L : (h + 1) * L],
                wide[:, h * TILE : (h + 1) * TILE],
                preferred_element_type=F32,
            )
            for h in range(heads)
        ],
        axis=0,
    )
    return out.T.astype(BF)


def predict_kernel(
    lengths_ref,
    tsub_ref,
    dsub_ref,
    tokens_ref,
    towner_ref,
    downer_ref,
    embedding_ref,
    code_ref,
    w_qkv_ref,
    w_out_ref,
    w_up_ref,
    w_down_ref,
    gain_ref,
    final_ref,
    w_head_ref,
    rows_ref,
    logit_ref,
):
    peps = STEP // L
    first = pl.program_id(0) * peps
    tokens = tokens_ref[0]
    onehot = (row_iota((32, STEP)) == tokens).astype(BF)
    state = lax.dot_general(onehot, embedding_ref[...], TN, preferred_element_type=F32)
    state = state + jnp.concatenate([code_ref[...]] * peps, axis=0)

    tile_lengths = []
    for t in range(STEP // TILE):
        lane = lane_iota((1, TILE)) // L
        vec = jnp.full((1, TILE), lengths_ref[first + t * 4], jnp.int32)
        for j in range(1, TILE // L):
            vec = jnp.where(lane == j, lengths_ref[first + t * 4 + j], vec)
        tile_lengths.append(vec)

    for layer in range(NL):
        normed = norm_rows(state, gain_ref[layer, 0:1, :].astype(F32))
        mixed = [
            jnp.dot(
                normed, w_qkv_ref[layer, :, c * D : (c + 1) * D], preferred_element_type=F32
            ).astype(BF)
            for c in range(3)
        ]
        tiles = []
        for t in range(STEP // TILE):
            parts = []
            for g in range(D // TILE):
                q, k, v = [
                    m[t * TILE : (t + 1) * TILE, g * TILE : (g + 1) * TILE] for m in mixed
                ]
                parts.append(attend(q, k, v, tile_lengths[t]))
            tiles.append(jnp.concatenate(parts, axis=1))
        attended = jnp.concatenate(tiles, axis=0)
        state = state + jnp.dot(attended, w_out_ref[layer], preferred_element_type=F32)
        normed = norm_rows(state, gain_ref[layer, 1:2, :].astype(F32))
        for c in range(FF // D):
            up = jnp.dot(
                normed, w_up_ref[layer, :, c * D : (c + 1) * D], preferred_element_type=F32
            )
            hidden = gelu(up).astype(BF)
            state = state + jnp.dot(
                hidden, w_down_ref[layer, c * D : (c + 1) * D, :], preferred_element_type=F32
            )
    normed = norm_rows(state, final_ref[...].astype(F32))
    head = jnp.concatenate([w_head_ref[...]] * 4, axis=1)
    logit_ref[...] = jnp.dot(normed, head, preferred_element_type=F32)

    lane = lane_iota((peps, 128)) // ION
    tiles = []
    for t in range(SPEC // 128):
        tile = logit_ref[pl.ds(4 * t, peps, stride=L), :]
        for i in range(1, 4):
            tile = jnp.where(lane == i, logit_ref[pl.ds(4 * t + i, peps, stride=L), :], tile)
        tiles.append(tile)
    logits = jnp.concatenate(tiles, axis=1)
    intensity = 1.0 / (1.0 + jnp.exp(-logits))
    where_row = row_iota((peps, 128))
    length = jnp.zeros((peps, 128), jnp.int32)
    tsub = jnp.zeros((peps, 128), jnp.int32)
    dsub = jnp.zeros((peps, 128), jnp.int32)
    for i in range(peps):
        length = jnp.where(where_row == i, lengths_ref[first + i], length)
        tsub = jnp.where(where_row == i, tsub_ref[first + i], tsub)
        dsub = jnp.where(where_row == i, dsub_ref[first + i], dsub)
    position = lane_iota((peps, SPEC)) // ION
    length = jnp.concatenate([length] * (SPEC // 128), axis=1)
    intensity = jnp.where(position < length - 1, intensity, F32(0.0))
    start = pl.multiple_of(first, peps)
    rows_ref[:, :SPEC] = standardize(intensity)
    column = lane_iota((peps, 128))
    tag = jnp.where(column == 0, towner_ref[...], tsub)
    tag = jnp.where(column == 2, downer_ref[...], tag)
    tag = jnp.where(column == 3, dsub, tag)
    rows_ref[:, SPEC:] = tag.astype(F32).astype(BF)


def predict_rows(
    tokens, lengths, towner, tsub, downer, dsub, embedding, w_qkv, w_out, w_up, w_down, gains, final, w_head
):
    count = tokens.shape[0]
    peps = STEP // L
    steps = count // peps
    whole = lambda shape: pl.BlockSpec(shape, lambda i, *_: (0,) * len(shape))
    grid = pltpu.PrefetchScalarGridSpec(
        num_scalar_prefetch=3,
        grid=(steps,),
        in_specs=[
            pl.BlockSpec((1, 1, STEP), lambda i, *_: (i, 0, 0)),
            pl.BlockSpec((peps, 1), lambda i, *_: (i, 0)),
            pl.BlockSpec((peps, 1), lambda i, *_: (i, 0)),
            whole(embedding.shape),
            whole((L, D)),
            whole(w_qkv.shape),
            whole(w_out.shape),
            whole(w_up.shape),
            whole(w_down.shape),
            whole(gains.shape),
            whole((1, D)),
            whole(w_head.shape),
        ],
        out_specs=pl.BlockSpec((peps, ROWW), lambda i, *_: (i, 0)),
        scratch_shapes=[pltpu.VMEM((STEP, 128), F32)],
    )
    return pl.pallas_call(
        predict_kernel,
        grid_spec=grid,
        out_shape=jax.ShapeDtypeStruct((count, ROWW), BF),
        compiler_params=pltpu.CompilerParams(vmem_limit_bytes=40 * 1024 * 1024),
        name="predict",
    )(
        lengths,
        tsub,
        dsub,
        tokens.reshape(steps, 1, STEP),
        towner,
        downer,
        embedding,
        jnp.asarray(sinusoid()),
        w_qkv,
        w_out,
        w_up,
        w_down,
        gains,
        final.reshape(1, D),
        w_head,
    )


def slots_of(bins):
    count = bins.shape[1]
    across = jnp.broadcast_to(bins.astype(F32), (count, count))
    down = across.T
    earlier = (across == down) & (row_iota((count, count)) < lane_iota((count, count)))
    rank = jnp.sum(earlier.astype(F32), axis=0, keepdims=True)
    local = bins.astype(F32) - jnp.min(bins.astype(F32), axis=1, keepdims=True)
    return (local * QPB + rank).astype(jnp.int32)


def query_kernel(bins_ref, spectra_ref, out_ref):
    count = spectra_ref.shape[0]
    place = (row_iota((count, count)) == slots_of(bins_ref[...])).astype(BF)
    ready = standardize(spectra_ref[...].astype(F32))
    out_ref[...] = jnp.dot(place, ready, preferred_element_type=F32).astype(BF)


def prepare_queries(query_bin, spectra):
    count = spectra.shape[0]
    return pl.pallas_call(
        query_kernel,
        out_shape=jax.ShapeDtypeStruct(spectra.shape, BF),
        name="prepare",
    )(query_bin.reshape(1, count), spectra)


QBLOCK = 256


def score_kernel(me_ref, queries_ref, *refs):
    sources, out_ref = refs[:-1], refs[-1]
    rows = jnp.concatenate([ref[:, :SPEC] for ref in sources], axis=0)
    tags = jnp.concatenate([ref[:, SPEC:] for ref in sources], axis=0).astype(F32)
    queries = queries_ref[...]
    turn = (
        row_iota((128, 128)) // ION * ION + lane_iota((128, 128)) % ION
        == (3 - lane_iota((128, 128)) // ION) * ION + lane_iota((128, 128)) % ION
    ) & (row_iota((128, 128)) % ION == lane_iota((128, 128)) % ION)
    turn = turn.astype(BF)
    tiles = SPEC // 128
    turned = jnp.concatenate(
        [
            jnp.dot(
                queries[:, (tiles - 1 - t) * 128 : (tiles - t) * 128], turn, preferred_element_type=F32
            ).astype(BF)
            for t in range(tiles)
        ],
        axis=1,
    )
    me = me_ref[0].astype(F32)
    first = pl.program_id(0) * (QBLOCK // QPB)
    bins = (lane_iota((1, QBLOCK)) // QPB + first).astype(F32)
    best = []
    for kind, side in enumerate((queries, turned)):
        scores = lax.dot_general(rows, side, NT, preferred_element_type=F32)
        sub = jnp.where(tags[:, 2 * kind : 2 * kind + 1] == me, tags[:, 2 * kind + 1 : 2 * kind + 2], F32(-1.0))
        scores = jnp.where(sub == bins, scores, F32(0.0))
        best.append(jnp.max(scores, axis=0, keepdims=True) * F32(1.0 / math.sqrt(SPEC)))
    lane = lane_iota((8, 128))
    row = row_iota((8, 128))
    out = jnp.zeros((8, 128), F32)
    for s in range(QBLOCK // 32):
        tile, shift = s // 4, 32 * (s % 4)
        pair = [jnp.broadcast_to(b[:, tile * 128 : (tile + 1) * 128], (8, 128)) for b in best]
        near = pltpu.roll(pair[0], (128 - shift) % 128, 1)
        far = pltpu.roll(pair[1], (128 - shift + 32) % 128, 1)
        out = jnp.where(row == s, jnp.where(lane < 32, near, far), out)
    out_ref[...] = out


def score(me, queries, sources):
    blocks = queries.shape[0] // QBLOCK
    count = sources[0].shape[0]
    return pl.pallas_call(
        score_kernel,
        grid=(blocks,),
        in_specs=[
            pl.BlockSpec(memory_space=pltpu.SMEM),
            pl.BlockSpec((QBLOCK, SPEC), lambda i: (i, 0)),
        ]
        + [pl.BlockSpec((count, ROWW), lambda i: (0, 0))] * len(sources),
        out_specs=pl.BlockSpec((QBLOCK // 32, 128), lambda i: (i, 0)),
        out_shape=jax.ShapeDtypeStruct((queries.shape[0] // 32, 128), F32),
        compiler_params=pltpu.CompilerParams(vmem_limit_bytes=40 * 1024 * 1024),
        name="score",
    )(me, queries, *sources)


def finish_kernel(bins_ref, pieces_ref, target_ref, decoy_ref):
    count = bins_ref.shape[1]
    best = jnp.maximum(jnp.max(pieces_ref[...], axis=0, keepdims=True), F32(0.0))
    slots = slots_of(bins_ref[...])
    place = row_iota((count, count)) == slots
    for kind, ref in enumerate((target_ref, decoy_ref)):
        wide = jnp.broadcast_to(best[:, kind * count : (kind + 1) * count], (count, count)).T
        ref[...] = jnp.sum(jnp.where(place, wide, F32(0.0)), axis=0, keepdims=True)


def finish(query_bin, pieces):
    count = query_bin.shape[0]
    shape = jax.ShapeDtypeStruct((1, count), F32)
    target, decoy = pl.pallas_call(finish_kernel, out_shape=(shape, shape), name="finish")(
        query_bin.reshape(1, count), pieces
    )
    return target.reshape(count), decoy.reshape(count)


def local(
    xs,
    ys,
    zs,
    peptide_tokens,
    peptide_lengths,
    target_owner,
    target_sub,
    decoy_owner,
    decoy_sub,
    embedding,
    w_qkv,
    w_out,
    w_up,
    w_down,
    layer_gain,
    final_gain,
    w_head,
    query_spectra,
    query_bin,
):
    along_z = [[y * zs + z for z in range(zs)] for y in range(ys)]
    along_y = [[y * zs + z for y in range(ys)] for z in range(zs)]
    queries = prepare_queries(query_bin, query_spectra)
    queries = lax.all_gather(queries, "seq", axis=0, tiled=True, axis_index_groups=along_z)
    queries = lax.all_gather(queries, "seq", axis=0, tiled=True, axis_index_groups=along_y)
    rows = predict_rows(
        peptide_tokens,
        peptide_lengths,
        target_owner,
        target_sub,
        decoy_owner,
        decoy_sub,
        embedding,
        w_qkv,
        w_out,
        w_up,
        w_down,
        layer_gain,
        final_gain,
        w_head,
    )
    swap = [(i, i ^ 1) for i in range(2 * xs)]
    held = [rows] + [
        lax.ppermute(rows, "mass", [(i, (i + 2 * d) % (2 * xs)) for i in range(2 * xs)])
        for d in range(1, xs)
    ]
    held = held + [lax.ppermute(part, "mass", swap) for part in held]
    me = lax.axis_index("mass").astype(jnp.int32).reshape(1)
    pieces = score(me, queries, held)
    pieces = lax.all_to_all(pieces, "seq", split_axis=0, concat_axis=0, tiled=True)
    return finish(query_bin, pieces)


def solution(mesh):
    in_specs = (
        P(("mass", "seq"), None),
        P(("mass", "seq")),
        P(("mass", "seq"), None),
        P(("mass", "seq")),
        P(("mass", "seq"), None),
        P(("mass", "seq")),
        P(),
        P(),
        P(),
        P(),
        P(),
        P(),
        P(),
        P(),
        P(("mass", "seq"), None),
        P(("mass", "seq")),
    )
    out_specs = (P(("mass", "seq")), P(("mass", "seq")))
    body = functools.partial(local, mesh.shape["mass"] // 2, 4, mesh.shape["seq"] // 4)
    return jax.shard_map(body, mesh=mesh, in_specs=in_specs, out_specs=out_specs, check_vma=False)
```

time: 378 us -> 134 us (0.35)
  waiting for transfers between devices: 98.3 us -> 1.03 us
  local copies, waits for them, and re-layouts: 85.4 us -> 12.9 us
  matrix products: 61.1 us -> 0 us
  blocking collectives: 91.1 us -> 42.7 us
  Pallas kernels: 0 us -> 47 us
  other arithmetic: 17.8 us -> 0 us
  starting transfers between devices: 8.2 us -> 15.6 us
    all_gather x2 -> x1, waiting for transfers between devices: 91.4 us -> 0.01 us  [local(): lax.all_gather(queries, 'seq', axis=0, tiled=True, axis_index_groups=alon...]
    dot_general x16 -> x0, matrix products: 61.1 us -> none  [the longest x2 14.5 us: predict_block(): jnp.einsum('phqk,pkhe->pqhe', probs, mixed[:, :, 2], preferred_element_ty...]
    pallas_call x0 -> x4, Pallas kernels: none -> 47 us  [the longest x1 39.7 us: predict_rows(): pl.pallas_call(predict_kernel, grid_spec=grid, out_shape=jax.ShapeDtypeSt...]
    all_gather x2 -> x1, blocking collectives: 67.7 us -> 26.5 us  [local(): lax.all_gather(queries, 'seq', axis=0, tiled=True, axis_index_groups=alon...]
    reshape x7 -> x2, local copies, waits for them, and re-layouts: 37 us -> 0.74 us  [the longest x1 0.66 us: predict_rows(): final.reshape(1, D)]
    slice x2 -> x0, local copies, waits for them, and re-layouts: 16 us -> none  [predict_block(): mixed[:, :, 2]]
    ppermute x0 -> x7, starting transfers between devices: none -> 15.6 us  [the longest x4 10.7 us: local(): held = held + [lax.ppermute(part, 'mass', swap) for part in held]]
    convert_element_type x2 -> x0, local copies, waits for them, and re-layouts: 13.2 us -> none  [predict_block(): attended = jnp.einsum('phqk,pkhe->pqhe', probs, mixed[:, :, 2], preferred...]
  transfers between devices with their start and end apart: 4 -> 8, of which waited for: 3 -> 2; matrix products, arithmetic and copies ran while one was open for 3% -> 3% of each run, Pallas kernels for 0% -> 30%
where the time goes in v1:
time: 134 us; the launch traced here: 133 us
  Pallas kernels  47 us (35%)
  blocking collectives  42.7 us (32%)
  starting transfers between devices  15.6 us (12%)
  between operations  14.1 us (11%)
  local copies, waits for them, and re-layouts  12.9 us (10%)
    pallas_call x1, Pallas kernels, predict_rows(): pl.pallas_call(predict_kernel, grid_spec=grid, out_shape=jax.ShapeDtypeSt...  39.7 us
    all_gather x1, blocking collectives, local(): lax.all_gather(queries, 'seq', axis=0, tiled=True, axis_index_groups=alon...  26.5 us
    all_to_all x1, blocking collectives, local(): lax.all_to_all(pieces, 'seq', split_axis=0, concat_axis=0, tiled=True)  16.2 us
    unnamed x26, local copies, waits for them, and re-layouts  12.1 us
    ppermute x4, starting transfers between devices, local(): held = held + [lax.ppermute(part, 'mass', swap) for part in held]  10.7 us
    ppermute x3, starting transfers between devices, local(): lax.ppermute(rows, 'mass', [(i, (i + 2 * d) % (2 * xs)) for i in range(2...  4.89 us
    pallas_call x1, Pallas kernels, score(): pl.pallas_call(score_kernel, grid=(blocks,), in_specs=[pl.BlockSpec(memor...  3.92 us
  transfers between devices with their start and end apart: 8, of which 2 were waited for; matrix products, arithmetic and copies ran while one was open for 3% of the time, Pallas kernels for 30%

profile of v1, /device:TPU:1, one launch (start us, length us, event | category | flops | bytes accessed | tf_op | source)
XLA Modules:
  0.0 133.2 jit_solution(10000650323571421334)
XLA Ops:
  7.2 0.0 copy-start.1
  7.2 0.0 all-gather.2.cloned.1.call-start
  7.2 1.9 %prepare.1 = bf16[32,1024]{1,0:T(8,128)(2,1)} custom-call(s32[1,32]{1,0:T(1,128)} %bitcast.10, bf16[32,1024]{1,0:T(8,128)(2,1)} %spectra_ref.1), custom_call_target="tpu_custom_call" | custom-call | tf_op jit(solution)/shard_map/prepare/pallas_call | solution.py:262
  9.1 26.5 %all_gather.6 = bf16[256,1024]{1,0:T(8,128)(2,1)} all-gather(bf16[32,1024]{1,0:T(8,128)(2,1)} %prepare.1), channel_id=1, replica_groups={{0,1,2,3,4,5,6,7},{8,9,10,11,12,13,14,15},{16,17,18,19,20,21,22,23},{24..., dimensions={0}, use_global_device_ids=true | all-gather | bytes 589824 | tf_op jit(solution)/shard_map/all_gather | solution.py:374
  35.6 0.0 all-gather.2.cloned.1.call-update
  35.6 0.8 copy.28
  36.4 0.1 reshape.31.tokens_ref
  36.5 0.7 copy.30.towner_ref
  37.3 0.7 copy.31.downer_ref
  38.0 0.7 reshape.28.final_ref
  38.7 0.8 copy.32.w_head_ref
  39.5 0.0 copy-done.1
  39.5 0.0 copy-start.2
  39.5 1.2 copy-done.2
  40.7 0.0 copy-start.3
  40.7 1.1 copy-done.3
  41.9 0.0 copy-start.4
  41.9 0.9 copy-done.4
  42.8 0.0 copy-start.5
  42.8 0.8 copy-done.5
  43.6 0.0 copy-start.6
  43.6 0.7 copy-done.6
  44.3 0.0 copy-start.7
  44.3 0.7 copy-done.7
  45.0 0.0 copy-start.8
  45.0 0.7 copy-done.8
  45.6 0.0 copy-start.9
  45.6 0.7 copy-done.9
  46.3 0.0 copy-start.10
  46.3 0.7 copy-done.10
  46.9 39.7 %predict.1.refs_0_ = bf16[64,1152]{1,0:T(8,128)(2,1)S(1)} custom-call(s32[64]{0:T(128)S(1)} %copy-done.8, s32[64]{0:T(128)S(1)} %copy-done.9, s32[64]{0:T(128)S(1)} %copy-done.10, s32[8,1,256]{2,1,0:T(1,128)S(1)} %reshape.31.tokens_ref, s32[64,1]{1,0:T(8,128)S(1)} %copy.30.towner_ref, s32[64,1]{1,0:T(8,128)S(1)} %copy.31.downer_ref, ...), custom_call_target="tpu_custom_call" | custom-call | tf_op jit(solution)/shard_map/predict/pallas_call | solution.py:218
  86.7 1.3 collective-permute-start
  88.0 2.4 %collective-permute-start.1 = (bf16[64,1152]{1,0:T(8,128)(2,1)S(1)}, bf16[64,1152]{1,0:T(8,128)(2,1)S(1)}, u32[]{:S(2)}, u32[]{:S(2)}) collective-permute-start(bf16[64,1152]{1,0:T(8,128)(2,1)S(1)} %predict.1.refs_0_), channel_id=1, source_target_pairs={{0,128},{32,160},{64,192},{96,224},{128,0},{160,32},{192,64},{224,... | collective-permute-start | bytes 442376 | tf_op jit(solution)/shard_map/ppermute | solution.py:394
  90.4 1.2 collective-permute-start.2
  91.6 7.0 %collective-permute-start.3 = (bf16[64,1152]{1,0:T(8,128)(2,1)S(1)}, bf16[64,1152]{1,0:T(8,128)(2,1)S(1)}, u32[]{:S(2)}, u32[]{:S(2)}) collective-permute-start(bf16[64,1152]{1,0:T(8,128)(2,1)S(1)} %predict.1.refs_0_), channel_id=1, source_target_pairs={{0,32},{32,0},{64,96},{96,64},{128,160},{160,128},{192,224},{224,1... | collective-permute-start | bytes 442376 | tf_op jit(solution)/shard_map/ppermute | solution.py:397
  98.6 0.0 collective-permute-done.refs_1_
  98.6 0.7 collective-permute-start.4
  99.2 0.0 collective-permute-done.1.refs_2_
  99.2 2.6 %collective-permute-start.5 = (bf16[64,1152]{1,0:T(8,128)(2,1)S(1)}, bf16[64,1152]{1,0:T(8,128)(2,1)S(1)}, u32[]{:S(2)}, u32[]{:S(2)}) collective-permute-start(bf16[64,1152]{1,0:T(8,128)(2,1)S(1)} %collective-permute-done.1.refs_2_), channel_id=1, source_target_pairs={{0,32},{32,0},{64,96},{96,64},{128,160},{160,128},{192,224},{224,1... | collective-permute-start | bytes 442376 | tf_op jit(solution)/shard_map/ppermute | solution.py:397
  101.8 0.0 collective-permute-done.2.refs_3_
  101.8 0.4 collective-permute-start.6
  102.3 0.0 collective-permute-done.3.refs_4_
  102.3 0.0 collective-permute-done.4.refs_5_
  102.3 0.6 collective-permute-done.5.refs_6_
  102.8 0.4 collective-permute-done.6.refs_7_
  103.3 0.0 all-gather.2.cloned.1.call-done.queries_ref
  103.3 0.0 copy-start
  103.3 1.6 %copy-done = bf16[1024,1024]{1,0:T(8,128)(2,1)S(1)} copy-done((bf16[1024,1024]{1,0:T(8,128)(2,1)S(1)}, bf16[1024,1024]{1,0:T(8,128)(2,1)}, u32[]{:S(2)}) %copy-start) | copy-done | bytes 2097176
  104.9 3.9 %score.1 = f32[32,128]{1,0:T(8,128)S(1)} custom-call(s32[1]{0:T(128)} %bitcast.1.me_ref, bf16[1024,1024]{1,0:T(8,128)(2,1)S(1)} %copy-done, bf16[64,1152]{1,0:T(8,128)(2,1)S(1)} %predict.1.refs_0_, bf16[64,1152]{1,0:T(8,128)(2,1)S(1)} %collective-permute-done.refs_1_, bf16[64,1152]{1,0:T(8,128)(2,1)S(1)} %collective-permute-done.1.refs_2_, ...), custom_call_target="tpu_custom_call" | custom-call | tf_op jit(solution)/shard_map/score/pallas_call | solution.py:316
  108.8 16.2 %all_to_all.11 = f32[32,1,128]{2,1,0:T(1,128)} all-to-all(f32[32,1,128]{2,1,0:T(1,128)S(1)} %bitcast.8), channel_id=1, replica_groups=mesh['mass'=8,'seq'=32] {'seq'}, dimensions={0} | all-to-all | bytes 32768 | tf_op jit(solution)/shard_map/all_to_all | solution.py:400
  125.0 1.4 %finish.1 = (f32[1,32]{1,0:T(1,128)}, f32[1,32]{1,0:T(1,128)}) custom-call(s32[1,32]{1,0:T(1,128)} %bitcast.11, f32[32,128]{1,0:T(8,128)} %bitcast.9), custom_call_target="tpu_custom_call" | custom-call | tf_op jit(solution)/shard_map/finish/pallas_call | solution.py:344
Async XLA Ops:
  7.2 32.3 %copy-start.1 = (bf16[2,256,1024]{2,1,0:T(8,128)(2,1)S(1)}, bf16[2,256,1024]{2,1,0:T(8,128)(2,1)}, u32[]{:S(2)}) copy-start(bf16[2,256,1024]{2,1,0:T(8,128)(2,1)} %w_up_ref.1) | copy-start | bytes 3145732
  7.2 96.1 %all-gather.2.cloned.1.call-start = ((), (), s32[]{:S(2)}) async-start(), calls=%async_computation.1 | async-start | bytes 2621440 | tf_op jit(solution)/shard_map/all_gather | solution.py:375
  39.5 1.2 copy-start.2
  40.7 1.1 copy-start.3
  41.9 0.9 copy-start.4
  42.8 0.8 copy-start.5
  43.6 0.7 copy-start.6
  44.3 0.7 copy-start.7
  45.0 0.7 copy-start.8
  45.6 0.7 copy-start.9
  46.3 0.7 copy-start.10
  86.7 11.9 %collective-permute-start = (bf16[64,1152]{1,0:T(8,128)(2,1)S(1)}, bf16[64,1152]{1,0:T(8,128)(2,1)S(1)}, u32[]{:S(2)}, u32[]{:S(2)}) collective-permute-start(bf16[64,1152]{1,0:T(8,128)(2,1)S(1)} %predict.1.refs_0_), channel_id=1, source_target_pairs={{0,64},{32,96},{64,128},{96,160},{128,192},{160,224},{192,0},{224,... | collective-permute-start | bytes 442376 | tf_op jit(solution)/shard_map/ppermute | solution.py:394
  88.0 11.3 %collective-permute-start.1 = (bf16[64,1152]{1,0:T(8,128)(2,1)S(1)}, bf16[64,1152]{1,0:T(8,128)(2,1)S(1)}, u32[]{:S(2)}, u32[]{:S(2)}) collective-permute-start(bf16[64,1152]{1,0:T(8,128)(2,1)S(1)} %predict.1.refs_0_), channel_id=1, source_target_pairs={{0,128},{32,160},{64,192},{96,224},{128,0},{160,32},{192,64},{224,... | collective-permute-start | bytes 442376 | tf_op jit(solution)/shard_map/ppermute | solution.py:394
  90.4 11.4 %collective-permute-start.2 = (bf16[64,1152]{1,0:T(8,128)(2,1)S(1)}, bf16[64,1152]{1,0:T(8,128)(2,1)S(1)}, u32[]{:S(2)}, u32[]{:S(2)}) collective-permute-start(bf16[64,1152]{1,0:T(8,128)(2,1)S(1)} %predict.1.refs_0_), channel_id=1, source_target_pairs={{0,192},{32,224},{64,0},{96,32},{128,64},{160,96},{192,128},{224,1... | collective-permute-start | bytes 442376 | tf_op jit(solution)/shard_map/ppermute | solution.py:394
  91.6 10.7 %collective-permute-start.3 = (bf16[64,1152]{1,0:T(8,128)(2,1)S(1)}, bf16[64,1152]{1,0:T(8,128)(2,1)S(1)}, u32[]{:S(2)}, u32[]{:S(2)}) collective-permute-start(bf16[64,1152]{1,0:T(8,128)(2,1)S(1)} %predict.1.refs_0_), channel_id=1, source_target_pairs={{0,32},{32,0},{64,96},{96,64},{128,160},{160,128},{192,224},{224,1... | collective-permute-start | bytes 442376 | tf_op jit(solution)/shard_map/ppermute | solution.py:397
  98.6 3.7 %collective-permute-start.4 = (bf16[64,1152]{1,0:T(8,128)(2,1)S(1)}, bf16[64,1152]{1,0:T(8,128)(2,1)S(1)}, u32[]{:S(2)}, u32[]{:S(2)}) collective-permute-start(bf16[64,1152]{1,0:T(8,128)(2,1)S(1)} %collective-permute-done.refs_1_), channel_id=1, source_target_pairs={{0,32},{32,0},{64,96},{96,64},{128,160},{160,128},{192,224},{224,1... | collective-permute-start | bytes 442376 | tf_op jit(solution)/shard_map/ppermute | solution.py:397
  99.2 3.6 %collective-permute-start.5 = (bf16[64,1152]{1,0:T(8,128)(2,1)S(1)}, bf16[64,1152]{1,0:T(8,128)(2,1)S(1)}, u32[]{:S(2)}, u32[]{:S(2)}) collective-permute-start(bf16[64,1152]{1,0:T(8,128)(2,1)S(1)} %collective-permute-done.1.refs_2_), channel_id=1, source_target_pairs={{0,32},{32,0},{64,96},{96,64},{128,160},{160,128},{192,224},{224,1... | collective-permute-start | bytes 442376 | tf_op jit(solution)/shard_map/ppermute | solution.py:397
  101.8 1.5 %collective-permute-start.6 = (bf16[64,1152]{1,0:T(8,128)(2,1)S(1)}, bf16[64,1152]{1,0:T(8,128)(2,1)S(1)}, u32[]{:S(2)}, u32[]{:S(2)}) collective-permute-start(bf16[64,1152]{1,0:T(8,128)(2,1)S(1)} %collective-permute-done.2.refs_3_), channel_id=1, source_target_pairs={{0,32},{32,0},{64,96},{96,64},{128,160},{160,128},{192,224},{224,1... | collective-permute-start | bytes 442376 | tf_op jit(solution)/shard_map/ppermute | solution.py:397
  103.3 1.6 %copy-start = (bf16[1024,1024]{1,0:T(8,128)(2,1)S(1)}, bf16[1024,1024]{1,0:T(8,128)(2,1)}, u32[]{:S(2)}) copy-start(bf16[1024,1024]{1,0:T(8,128)(2,1)} %all-gather.2.cloned.1.call-done.queries_ref) | copy-start | bytes 6291460
Sparse Core Ops, SparseCore 0:
  35.7 38.4 all-gather.1
